TPU v7x, 32 devices: a whole 2x2x4 slice. The times are simulated.
32 devices in a mesh: segment: 4 (over y, x), feat: 4 (over z), tok: 2 (over core).
Axes of the slice: x: 2, y: 2, z: 4, core: 2. Of those that a mesh axis runs over, the one named last changes fastest.
Arguments:
- layer_inputs: bfloat16 [4, 448, 2304], P('segment', 'feat', 'tok'), may hold values from -6 to 6
- targets: bfloat16 [4, 448, 2304], P('segment', 'tok', 'feat'), may hold values from -6 to 6
- enc_weight: bfloat16 [4, 2304, 12288], P('segment', 'feat', 'tok'), may hold values from -0.125 to 0.125
- enc_bias: float32 [4, 12288], P('segment', 'tok'), may hold values from -3 to 3
- dec_weight: bfloat16 [4, 4, 2304, 12288], P('segment', None, 'feat', 'tok'), may hold values from -0.0546875 to 0.0546875
Outputs:
- features: bfloat16 [4, 448, 12288], P('segment', 'feat', 'tok')
- residual: float32 [4, 448, 2304], P('segment', 'tok', 'feat')
All inputs are finite; a program needn't handle non-finite values.
Results may differ from a plain program's by a relative error of at most 0.01.
Values may be sent and summed in bfloat16 or wider, within the bound.
No kernel may reach another device: no remote copies, remote signals or barrier semaphores. Data moves between devices by JAX's collectives and lax.ppermute only.
A program may use at most 128 MiB of HBM per device.

v0:
```python
import jax
import jax.numpy as jnp
from jax import lax
from jax.sharding import PartitionSpec as P


def local(layer_inputs, targets, enc_weight, enc_bias, dec_weight):
    segment_index = lax.axis_index("segment")
    full_rows = lax.all_gather(layer_inputs[0], "tok", axis=1, tiled=True)
    preact = jnp.dot(
        full_rows,
        lax.all_gather(enc_weight[0], "feat", axis=0, tiled=True),
        preferred_element_type=jnp.float32,
    )
    features = jax.nn.relu(preact + enc_bias[0][None, :]).astype(jnp.bfloat16)
    all_codes = lax.all_gather(features, "feat", axis=0, tiled=True)
    decoders = dec_weight[0]
    layers = decoders.shape[0]
    target_mask = (jnp.arange(layers) >= segment_index).astype(jnp.float32)
    decoded = jnp.einsum("nf,ldf->nld", all_codes, decoders, preferred_element_type=jnp.float32)
    contrib = lax.psum_scatter(
        (decoded * target_mask[None, :, None]).astype(jnp.bfloat16),
        "tok",
        scatter_dimension=0,
        tiled=True,
    ).astype(jnp.float32)
    routed = lax.all_to_all(
        contrib.astype(jnp.bfloat16), "segment", split_axis=1, concat_axis=1, tiled=True
    ).astype(contrib.dtype)
    own_recon = jnp.sum(routed, axis=1)
    residual = targets[0].astype(jnp.float32) - own_recon
    return (features[None], residual[None])


def solution(mesh):
    in_specs = (
        P("segment", "feat", "tok"),
        P("segment", "tok", "feat"),
        P("segment", "feat", "tok"),
        P("segment", "tok"),
        P("segment", None, "feat", "tok"),
    )
    out_specs = (P("segment", "feat", "tok"), P("segment", "tok", "feat"))
    return jax.shard_map(local, mesh=mesh, in_specs=in_specs, out_specs=out_specs, check_vma=False)
```

profile of v0, /device:TPU:0, one launch (start us, length us, event | category | flops | bytes accessed | tf_op | source)
XLA Modules:
  0.0 662.8 jit_solution(9816748495184017431)
XLA Ops:
  7.2 0.0 copy-start.1
  7.2 0.0 copy-start.2
  7.2 0.0 all-gather.7.cloned.1.call-start
  7.2 0.7 all-gather.7.cloned.1.call-update
  7.9 0.0 all-gather.5.cloned.1.call-start
  8.0 0.1 copy-done.1
  8.1 2.2 all-gather
  10.4 478.1 %all-gather.7.cloned.1.call-done = bf16[1,2304,6144]{2,1,0:T(8,128)(2,1)} async-done(((bf16[1,576,6144]{2,1,0:T(8,128)(2,1)}), bf16[1,2304,6144]{2,1,0:T(8,128)(2,1)}) %all-gather.7.cloned.1.call-update) | async-done | bytes 28311568 | tf_op jit(solution)/shard_map/all_gather | solution.py:12
  488.5 0.0 copy-done.2
  488.5 14.7 %fusion.10 = bf16[112,6144]{1,0:T(8,128)(2,1)} fusion(bf16[1,2304,6144]{2,1,0:T(8,128)(2,1)} %all-gather.7.cloned.1.call-done, f32[6144]{0:T(1024)S(1)} %bitcast.27, bf16[1,112,2304]{2,1,0:T(8,128)(2,1)S(1)} %all-gather), kind=kOutput, calls=%fused_computation.6 | convolution fusion | flops 3172958208 | bytes 30228480 | tf_op jit(solution)/shard_map/dot_general | solution.py:10
  503.2 0.0 all-gather.5.cloned.1.call-update
  503.2 0.0 reduce-scatter.2.cloned.1.call-start
  503.3 100.7 %all-gather.5.cloned.1.call-done = bf16[448,6144]{1,0:T(8,128)(2,1)} async-done(((bf16[112,6144]{1,0:T(8,128)(2,1)}), bf16[448,6144]{1,0:T(8,128)(2,1)}) %all-gather.5.cloned.1.call-update) | async-done | bytes 5505040 | tf_op jit(solution)/shard_map/all_gather | solution.py:16
  603.9 23.3 %multiply_convert_fusion = bf16[448,4,576]{2,0,1:T(8,128)(2,1)} fusion(f32[4]{0:T(128)S(1)} %compare_convert_fusion, bf16[1,4,576,6144]{3,2,1,0:T(8,128)(2,1)} %param.9, bf16[448,6144]{1,0:T(8,128)(2,1)} %all-gather.5.cloned.1.call-done), kind=kOutput, calls=%fused_computation.8 | convolution fusion | flops 12685639680 | bytes 35880976 | tf_op jit(solution)/shard_map/nf,ldf->nld/dot_general | solution.py:20
  627.2 0.0 copy-start
  627.2 0.0 reduce-scatter.2.cloned.1.call-update
  627.2 8.3 %reduce-scatter.2.cloned.1.call-done = bf16[224,4,576]{2,0,1:T(8,128)(2,1)} async-done(((bf16[448,4,576]{2,0,1:T(8,128)(2,1)}), bf16[224,4,576]{2,0,1:T(8,128)(2,1)}) %reduce-scatter.2.cloned.1.call-update) | async-done | bytes 1032208 | tf_op jit(solution)/shard_map/reduce_scatter | solution.py:21
  635.6 19.6 %all_to_all.5 = bf16[224,4,576]{2,0,1:T(8,128)(2,1)S(1)} all-to-all(bf16[224,4,576]{2,0,1:T(8,128)(2,1)} %reduce-scatter.2.cloned.1.call-done), channel_id=1, replica_groups=mesh['segment'=4,'feat'=4,'tok'=2] {'segment'}, dimensions={1} | all-to-all | bytes 2064384 | tf_op jit(solution)/shard_map/all_to_all | solution.py:27
  655.2 0.2 convert_reduce_fusion
  655.4 0.0 copy-done
  655.4 0.9 bitcast_subtract_fusion
  (1 shorter events, 0.0 us)
Async XLA Ops:
  7.2 0.9 copy-start.1
  7.2 481.3 %copy-start.2 = (f32[1,6144]{1,0:T(1,128)S(1)}, f32[1,6144]{1,0:T(1,128)}, u32[]{:S(2)}) copy-start(f32[1,6144]{1,0:T(1,128)} %param.8) | copy-start | bytes 73732
  7.2 481.3 %all-gather.7.cloned.1.call-start = ((), (), s32[]{:S(2)}) async-start(), calls=%async_computation.4 | async-start | bytes 35389440 | tf_op jit(solution)/shard_map/all_gather | solution.py:12
  7.9 596.0 %all-gather.5.cloned.1.call-start = ((), (), s32[]{:S(2)}) async-start(), calls=%async_computation.2 | async-start | bytes 6881280 | tf_op jit(solution)/shard_map/all_gather | solution.py:16
  503.2 132.4 %reduce-scatter.2.cloned.1.call-start = ((), (), s32[]{:S(2)}) async-start(), calls=%async_computation.3 | async-start | bytes 3440640 | tf_op jit(solution)/shard_map/reduce_scatter | solution.py:21
  627.2 28.2 %copy-start = (bf16[1,224,576]{2,1,0:T(8,128)(2,1)S(1)}, bf16[1,224,576]{2,1,0:T(8,128)(2,1)}, u32[]{:S(2)}) copy-start(bf16[1,224,576]{2,1,0:T(8,128)(2,1)} %param.6) | copy-start | bytes 774148
Sparse Core Ops, SparseCore 0:
  9.6 478.8 all-gather.6
  503.3 100.5 all-gather.4
  627.3 8.1 reduce-scatter.1
where the time goes:
time: 663 us
  waiting for transfers between devices  588 us (89%)
  matrix products  38 us (6%)
  blocking collectives  21.9 us (3%)
  between operations  13.8 us (2%)
    all_gather x1, waiting for transfers between devices, local(): lax.all_gather(enc_weight[0], 'feat', axis=0, tiled=True)  478 us
    all_gather x1, waiting for transfers between devices, local(): all_codes = lax.all_gather(features, 'feat', axis=0, tiled=True)  101 us
    dot_general x1, matrix products, local(): jnp.einsum('nf,ldf->nld', all_codes, decoders, preferred_element_type=jnp...  23.3 us
    all_to_all x1, blocking collectives, local(): lax.all_to_all(contrib.astype(jnp.bfloat16), 'segment', split_axis=1, con...  19.6 us
    dot_general x1, matrix products, local(): jnp.dot(full_rows, lax.all_gather(enc_weight[0], 'feat', axis=0, tiled=Tr...  14.7 us
  transfers between devices with their start and end apart: 3, of which 3 were waited for; matrix products, arithmetic and copies ran while one was open for 0% of the time, Pallas kernels for 0%

commit v1 on v0

--- a/solution.py
+++ b/solution.py
@@ -6,12 +6,12 @@
 
 def local(layer_inputs, targets, enc_weight, enc_bias, dec_weight):
     segment_index = lax.axis_index("segment")
-    full_rows = lax.all_gather(layer_inputs[0], "tok", axis=1, tiled=True)
-    preact = jnp.dot(
-        full_rows,
-        lax.all_gather(enc_weight[0], "feat", axis=0, tiled=True),
-        preferred_element_type=jnp.float32,
-    )
+    rows = lax.all_gather(layer_inputs[0], "tok", axis=1, tiled=True)
+    columns = lax.all_to_all(rows, "feat", split_axis=1, concat_axis=0, tiled=True)
+    partial = jnp.dot(columns, enc_weight[0], preferred_element_type=jnp.float32)
+    preact = lax.psum_scatter(
+        partial.astype(jnp.bfloat16), "feat", scatter_dimension=0, tiled=True
+    ).astype(jnp.float32)
     features = jax.nn.relu(preact + enc_bias[0][None, :]).astype(jnp.bfloat16)
     all_codes = lax.all_gather(features, "feat", axis=0, tiled=True)
     decoders = dec_weight[0]

time: 663 us -> 303 us (0.46)
  waiting for transfers between devices: 588 us -> 222 us
    all_gather x1 -> x0, waiting for transfers between devices: 478 us -> none  [local(): lax.all_gather(enc_weight[0], 'feat', axis=0, tiled=True)]
    reduce_scatter x0 -> x1, waiting for transfers between devices: none -> 97.2 us  [local(): lax.psum_scatter(partial.astype(jnp.bfloat16), 'feat', scatter_dimension=...]
    all_to_all x0 -> x1, waiting for transfers between devices: none -> 13.7 us  [local(): lax.all_to_all(contrib.astype(jnp.bfloat16), 'segment', split_axis=1, con...]
  transfers between devices with their start and end apart: 3 -> 4, of which waited for: 3 -> 4; matrix products, arithmetic and copies ran while one was open for 0% -> 0% of each run, Pallas kernels for 0% -> 0%
where the time goes in v1:
time: 303 us
  waiting for transfers between devices  222 us (73%)
  matrix products  32.6 us (11%)
  blocking collectives  24.4 us (8%)
  between operations  13.8 us (5%)
  other arithmetic  5.21 us (2%)
  starting transfers between devices  4.01 us (1%)
    all_gather x1, waiting for transfers between devices, local(): all_codes = lax.all_gather(features, 'feat', axis=0, tiled=True)  103 us
    reduce_scatter x1, waiting for transfers between devices, local(): lax.psum_scatter(partial.astype(jnp.bfloat16), 'feat', scatter_dimension=...  97.2 us
    dot_general x1, matrix products, local(): jnp.einsum('nf,ldf->nld', all_codes, decoders, preferred_element_type=jnp...  23.3 us
    all_to_all x1, blocking collectives, local(): lax.all_to_all(rows, 'feat', split_axis=1, concat_axis=0, tiled=True)  21.9 us
    all_to_all x1, waiting for transfers between devices, local(): lax.all_to_all(contrib.astype(jnp.bfloat16), 'segment', split_axis=1, con...  13.7 us
    dot_general x1, matrix products, local(): jnp.dot(columns, enc_weight[0], preferred_element_type=jnp.float32)  9.34 us
    reduce_scatter x1, waiting for transfers between devices, local(): lax.psum_scatter((decoded * target_mask[None, :, None]).astype(jnp.bfloat...  8.33 us
  transfers between devices with their start and end apart: 4, of which 4 were waited for; matrix products, arithmetic and copies ran while one was open for 0% of the time, Pallas kernels for 0%

profile of v1, /device:TPU:0, one launch (start us, length us, event | category | flops | bytes accessed | tf_op | source)
XLA Modules:
  0.0 303.1 jit_solution(13598653967124940857)
XLA Ops:
  7.2 0.0 reduce-scatter.3.cloned.1.call-start
  7.2 2.5 all-gather
  9.7 0.7 all_to_all.17
  10.3 0.1 copy.8
  10.4 21.9 %all_to_all.24 = bf16[112,4,576]{2,0,1:T(8,128)(2,1)S(1)} all-to-all(bf16[112,4,576]{2,0,1:T(8,128)(2,1)S(1)} %copy.8), channel_id=1, replica_groups=mesh['segment'=4,'feat'=4,'tok'=2] {'feat'}, dimensions={1} | all-to-all | bytes 1032192 | tf_op jit(solution)/shard_map/all_to_all | solution.py:10
  32.3 9.3 %convolution_convert_fusion = bf16[448,6144]{1,0:T(8,128)(2,1)} fusion(bf16[448,576]{1,0:T(8,128)(2,1)S(1)} %bitcast.22, bf16[1,576,6144]{2,1,0:T(8,128)(2,1)} %param.7), kind=kOutput, calls=%fused_computation.2 | convolution fusion | flops 3173646336 | bytes 13099008 | tf_op jit(solution)/shard_map/dot_general | solution.py:11
  41.6 0.0 copy-start.2
  41.6 0.0 reduce-scatter.3.cloned.1.call-update
  41.7 0.0 all-gather.3.cloned.1.call-start
  41.7 97.2 %reduce-scatter.3.cloned.1.call-done = bf16[112,6144]{1,0:T(8,128)(2,1)} async-done(((bf16[448,6144]{1,0:T(8,128)(2,1)}), bf16[112,6144]{1,0:T(8,128)(2,1)}) %reduce-scatter.3.cloned.1.call-update) | async-done | bytes 1376272 | tf_op jit(solution)/shard_map/reduce_scatter | solution.py:12
  138.9 0.0 copy-done.2
  139.0 2.8 maximum_convert_fusion
  141.7 0.0 all-gather.3.cloned.1.call-update
  141.7 0.0 reduce-scatter.5.cloned.1.call-start
  141.8 103.0 %all-gather.3.cloned.1.call-done = bf16[448,6144]{1,0:T(8,128)(2,1)} async-done(((bf16[112,6144]{1,0:T(8,128)(2,1)}), bf16[448,6144]{1,0:T(8,128)(2,1)}) %all-gather.3.cloned.1.call-update) | async-done | bytes 5505040 | tf_op jit(solution)/shard_map/all_gather | solution.py:16
  244.8 23.3 %multiply_convert_fusion = bf16[448,4,576]{2,0,1:T(8,128)(2,1)} fusion(f32[4]{0:T(128)S(1)} %compare_convert_fusion, bf16[1,4,576,6144]{3,2,1,0:T(8,128)(2,1)} %param.9, bf16[448,6144]{1,0:T(8,128)(2,1)} %all-gather.3.cloned.1.call-done), kind=kOutput, calls=%fused_computation.5 | convolution fusion | flops 12685639680 | bytes 35880976 | tf_op jit(solution)/shard_map/nf,ldf->nld/dot_general | solution.py:20
  268.1 0.0 copy-start
  268.1 0.0 reduce-scatter.5.cloned.1.call-update
  268.1 8.3 %reduce-scatter.5.cloned.1.call-done = bf16[224,4,576]{2,0,1:T(8,128)(2,1)} async-done(((bf16[448,4,576]{2,0,1:T(8,128)(2,1)}), bf16[224,4,576]{2,0,1:T(8,128)(2,1)}) %reduce-scatter.5.cloned.1.call-update) | async-done | bytes 1032208 | tf_op jit(solution)/shard_map/reduce_scatter | solution.py:21
  276.4 3.9 %all-to-all-start.1 = ((bf16[224,4,576]{2,0,1:T(8,128)(2,1)}), bf16[224,4,576]{2,0,1:T(8,128)(2,1)S(1)}, u32[]{:S(2)}, u32[]{:S(2)}) async-start(bf16[224,4,576]{2,0,1:T(8,128)(2,1)} %reduce-scatter.5.cloned.1.call-done), calls=%async_computation.3 | async-start | bytes 2293760 | tf_op jit(solution)/shard_map/all_to_all | solution.py:27
  280.3 0.0 copy-done
  280.3 0.0 copy-start.1
  280.3 1.4 fusion.9
  281.7 13.7 %all-to-all-done.1 = bf16[224,4,576]{2,0,1:T(8,128)(2,1)S(1)} async-done(((bf16[224,4,576]{2,0,1:T(8,128)(2,1)}), bf16[224,4,576]{2,0,1:T(8,128)(2,1)S(1)}, u32[]{:S(2)}, u32[]{:S(2)}) %all-to-all-start.1) | async-done | bytes 1032224 | tf_op jit(solution)/shard_map/all_to_all | solution.py:27
  295.5 0.2 convert_reduce_fusion
  295.7 0.0 copy-done.1
  295.7 0.9 bitcast_subtract_fusion
  (1 shorter events, 0.0 us)
Async XLA Ops:
  7.2 131.8 %reduce-scatter.3.cloned.1.call-start = ((), (), s32[]{:S(2)}) async-start(), calls=%async_computation.4 | async-start | bytes 6881280 | tf_op jit(solution)/shard_map/reduce_scatter | solution.py:12
  41.6 97.3 %copy-start.2 = (f32[1,6144]{1,0:T(1,128)S(1)}, f32[1,6144]{1,0:T(1,128)}, u32[]{:S(2)}) copy-start(f32[1,6144]{1,0:T(1,128)} %param.8) | copy-start | bytes 73732
  41.7 203.1 %all-gather.3.cloned.1.call-start = ((), (), s32[]{:S(2)}) async-start(), calls=%async_computation.5 | async-start | bytes 6881280 | tf_op jit(solution)/shard_map/all_gather | solution.py:16
  141.7 134.7 %reduce-scatter.5.cloned.1.call-start = ((), (), s32[]{:S(2)}) async-start(), calls=%async_computation.6 | async-start | bytes 3440640 | tf_op jit(solution)/shard_map/reduce_scatter | solution.py:21
  268.1 12.2 %copy-start = (bf16[112,6144]{1,0:T(8,128)(2,1)S(1)}, bf16[112,6144]{1,0:T(8,128)(2,1)}, u32[]{:S(2)}) copy-start(bf16[112,6144]{1,0:T(8,128)(2,1)} %reduce-scatter.3.cloned.1.call-done) | copy-start | bytes 4128772
  276.4 19.1 %all-to-all-start.1 = ((bf16[224,4,576]{2,0,1:T(8,128)(2,1)}), bf16[224,4,576]{2,0,1:T(8,128)(2,1)S(1)}, u32[]{:S(2)}, u32[]{:S(2)}) async-start(bf16[224,4,576]{2,0,1:T(8,128)(2,1)} %reduce-scatter.5.cloned.1.call-done), calls=%async_computation.3 | async-start | bytes 2293760 | tf_op jit(solution)/shard_map/all_to_all | solution.py:27
  280.3 15.3 %copy-start.1 = (bf16[1,224,576]{2,1,0:T(8,128)(2,1)S(1)}, bf16[1,224,576]{2,1,0:T(8,128)(2,1)}, u32[]{:S(2)}) copy-start(bf16[1,224,576]{2,1,0:T(8,128)(2,1)} %param.6) | copy-start | bytes 774148
Sparse Core Ops, SparseCore 0:
  41.8 97.1 reduce-scatter.2
  141.8 102.8 all-gather.2
  268.2 8.1 reduce-scatter.4
